TPU v7x, 256 devices: a whole 4x4x8 slice. The times are simulated.
256 devices in a mesh: row: 32 (over x, y, core), col: 8 (over z).
Axes of the slice: x: 4, y: 4, z: 8, core: 2. Of those that a mesh axis runs over, the one named last changes fastest.
Arguments:
- a_stored: bfloat16 [24576, 24576], P('row', 'col'), may hold values from -6 to 6
- pivots: int32 [2, 256], replicated, may hold values from 0 to 24575, as said below
- l_inverse: bfloat16 [2, 256, 256], replicated, as said below
- u_inverse: bfloat16 [2, 256, 256], replicated, as said below
Outputs:
- a_factored: bfloat16 [24576, 24576], P('row', 'col')
Inputs may be any that keep to these rules, and one draw needn't show every extreme that they name: `pivots`: for panel k, entry j is either k * 256 + j or a row at or after (k + 1) * 256; the entries of one panel are distinct; entry 0 of panel 0 is 0, entry 1 of panel k is global row (2) * 256 * 32 + ((k + 32 / 2) mod 32) * 256 + 256 / 2, and the last entry of each panel is 24575. `l_inverse`: lower triangular with unit diagonal. `u_inverse`: upper triangular with a positive diagonal.
All inputs are finite; a program needn't handle non-finite values.
Results may differ from a plain program's by a relative error of at most 0.0069.
Values may be sent and summed in bfloat16 or wider, within the bound.
A program may use at most 64 MiB of HBM per device.

v0:
```python
import jax
import jax.numpy as jnp
from jax import lax
from jax.sharding import PartitionSpec as P


def broadcast(array, axis, root):
    mine = lax.axis_index(axis) == root
    return lax.psum(jnp.where(mine, array, jnp.zeros_like(array)), axis)


def source_rows(pivots, section, panel_width, order):
    anchor = jnp.arange(order, dtype=jnp.int32)
    diagonal = section * panel_width + jnp.arange(panel_width, dtype=jnp.int32)
    anchor = anchor.at[pivots[section]].set(diagonal)
    return anchor.at[diagonal].set(pivots[section])


def leading_flags(targets):
    listed = targets.shape[0]
    equal = targets[:, None] == targets[None, :]
    earlier = jnp.arange(listed)[None, :] < jnp.arange(listed)[:, None]
    return jnp.logical_not(jnp.any(equal & earlier, axis=1))


def pick_rows(matrix, anchor, targets, my_row, row_count, panel_width):
    leading = leading_flags(targets)
    wanted = anchor[targets]
    owner = wanted // panel_width % row_count
    local_index = wanted // (panel_width * row_count) * panel_width + wanted % panel_width
    chosen = matrix[local_index]
    return jnp.where((leading & (owner == my_row))[:, None], chosen, jnp.zeros_like(chosen))


def place_rows(matrix, received, anchor, targets, glob_row):
    listed = targets.shape[0]
    order = anchor.shape[0]
    slot = (
        jnp.full((order,), listed, jnp.int32).at[targets].min(jnp.arange(listed, dtype=jnp.int32))
    )
    moved = anchor[glob_row] != glob_row
    arriving = received[jnp.minimum(slot[glob_row], listed - 1)]
    return jnp.where(moved[:, None], arriving, matrix)


def spread_upper(matrix, l_inverse, section, to_right):
    panel_width = l_inverse.shape[1]
    upper_part = jnp.dot(
        l_inverse[section], matrix[:panel_width], preferred_element_type=jnp.float32
    ).astype(jnp.bfloat16)
    values = jnp.where(to_right[None, :], upper_part, jnp.zeros_like(upper_part))
    return broadcast(values, "row", section)


def per_device(a_stored, pivots, l_inverse, u_inverse):
    matrix = a_stored
    rows_local, cols_local = matrix.shape
    panel_width = l_inverse.shape[1]
    row_count = lax.axis_size("row")
    col_count = lax.axis_size("col")
    my_row = lax.axis_index("row")
    my_col = lax.axis_index("col")
    order = rows_local * row_count
    row_local = jnp.arange(rows_local, dtype=jnp.int32)
    glob_row = (
        row_local // panel_width * panel_width * row_count
        + my_row * panel_width
        + row_local % panel_width
    )
    col_local = jnp.arange(cols_local, dtype=jnp.int32)
    glob_col = (
        col_local // panel_width * panel_width * col_count
        + my_col * panel_width
        + col_local % panel_width
    )
    for section in range(2):
        anchor = source_rows(pivots, section, panel_width, order)
        targets = jnp.concatenate(
            [section * panel_width + jnp.arange(panel_width, dtype=jnp.int32), pivots[section]]
        )
        picked = pick_rows(matrix, anchor, targets, my_row, row_count, panel_width)
        received = lax.psum(picked, "row").astype(jnp.float32).astype(jnp.bfloat16)
        matrix = place_rows(matrix, received, anchor, targets, glob_row)
        limit = (section + 1) * panel_width
        below = glob_row >= limit
        to_right = glob_col >= limit
        panel = matrix[:, :panel_width]
        lower_part = jnp.dot(panel, u_inverse[section], preferred_element_type=jnp.float32).astype(
            jnp.bfloat16
        )
        lower_values = jnp.where(below[:, None], lower_part, jnp.zeros_like(lower_part))
        lower_recv = broadcast(lower_values, "col", section)
        if section == 0:
            upper_recv = spread_upper(matrix, l_inverse, section, to_right)
        else:
            upper_recv = spread_upper(matrix, l_inverse, section, to_right)
        new_panel = jnp.where(below[:, None] & (my_col == section), lower_recv, panel)
        matrix = matrix.at[:, :panel_width].set(new_panel)
        top_rows = matrix[:panel_width]
        new_top = jnp.where(to_right[None, :] & (my_row == section), upper_recv, top_rows)
        matrix = matrix.at[:panel_width].set(new_top)
        product = jnp.dot(lower_recv, upper_recv, preferred_element_type=jnp.float32)
        trailing = below[:, None] & to_right[None, :]
        matrix = jnp.where(
            trailing, (matrix.astype(jnp.float32) - product).astype(jnp.bfloat16), matrix
        )
    return matrix


def solution(mesh):
    in_specs = (P("row", "col"), P(), P(), P())
    out_specs = P("row", "col")
    return jax.shard_map(
        per_device, mesh=mesh, in_specs=in_specs, out_specs=out_specs, check_vma=False
    )
```

profile of v0, /device:TPU:1, one launch (start us, length us, event | category | flops | bytes accessed | tf_op | source)
XLA Modules:
  0.0 731.7 jit_solution(10786084056398414659)
XLA Ops:
  6.5 0.0 all-reduce.7.cloned.1.call-start
  6.5 0.8 slice_bitcast_fusion.1
  7.3 0.8 compare_select_fusion.9
  8.1 0.2 fusion.17
  8.4 1.5 scatter_fusion.2
  9.9 1.5 scatter_fusion.3
  11.4 3.1 gather_fusion.3
  14.6 9.1 %gather_fusion.4 = bf16[512,3072]{1,0:T(8,128)(2,1)S(1)} fusion(bf16[768,3072]{1,0:T(8,128)(2,1)} %param.12, s32[1024]{0:T(1024)S(1)} %pad_clamp_fusion.3), kind=kCustom, calls=%fused_computation.4 | custom fusion | bytes 6293504 | tf_op jit(solution)/shard_map/gather | solution.py:31
  23.7 1.9 broadcast_select_fusion.2
  25.7 0.0 all-reduce.7.cloned.1.call-update
  25.7 0.0 all-reduce.9.cloned.1.call-start
  25.8 4.5 gather_fusion.2
  30.3 3.8 scatter_custom_fusion.4
  34.0 4.5 gather_fusion.5
  38.5 1.5 scatter_fusion
  40.0 1.7 scatter_fusion.1
  41.7 3.1 gather_fusion.1
  44.9 0.7 compare_reduce_fusion
  45.7 103.7 %all-reduce.7.cloned.1.call-done = bf16[512,3072]{1,0:T(8,128)(2,1)} async-done(((bf16[512,3072]{1,0:T(8,128)(2,1)}), bf16[512,3072]{1,0:T(8,128)(2,1)}) %all-reduce.7.cloned.1.call-update) | async-done | bytes 3145744 | tf_op jit(solution)/shard_map/psum | solution.py:82
  149.4 12.0 %gather_fusion.6 = bf16[768,3072]{1,0:T(8,128)(2,1)} fusion(bf16[512,3072]{1,0:T(8,128)(2,1)} %all-reduce.7.cloned.1.call-done, s32[1024]{0:T(1024)S(1)} %pad_clamp_fusion.2), kind=kCustom, calls=%fused_computation.6 | custom fusion | bytes 9440256 | tf_op jit(solution)/shard_map/gather | solution.py:42
  161.4 4.4 broadcast_select_fusion
  165.8 0.0 copy-start
  165.8 2.2 copy-done
  168.0 0.0 copy-done.6
  168.0 1.0 fusion.11
  169.0 0.0 all-reduce.9.cloned.1.call-update
  169.0 0.0 all-reduce.11.cloned.1.call-start
  169.1 0.0 copy-done.7
  169.1 3.1 fusion.5
  172.2 0.0 all-reduce.11.cloned.1.call-update
  172.3 0.0 all-reduce.13.cloned.1.call-start
  172.3 0.2 fusion.16
  172.6 64.9 %all-reduce.9.cloned.1.call-done = bf16[768,256]{1,0:T(8,128)(2,1)} async-done(((bf16[768,256]{1,0:T(8,128)(2,1)}), bf16[768,256]{1,0:T(8,128)(2,1)}) %all-reduce.9.cloned.1.call-update) | async-done | bytes 393232 | tf_op jit(solution)/shard_map/psum | solution.py:9
  237.5 2.9 fusion.18
  240.5 119.8 %all-reduce.11.cloned.1.call-done = bf16[256,3072]{1,0:T(8,128)(2,1)} async-done(((bf16[256,3072]{1,0:T(8,128)(2,1)}), bf16[256,3072]{1,0:T(8,128)(2,1)}) %all-reduce.11.cloned.1.call-update) | async-done | bytes 1572880 | tf_op jit(solution)/shard_map/psum | solution.py:9
  360.3 3.7 fusion.8
  364.0 0.0 copy-done.4
  364.0 0.0 copy-done.2
  364.0 7.9 %and_select_fusion = bf16[768,3072]{1,0:T(8,128)(2,1)} fusion(bf16[768,3072]{1,0:T(8,128)(2,1)} %fusion.8, bf16[768,256]{1,0:T(8,128)(2,1)S(1)} %copy-done.4, bf16[256,3072]{1,0:T(8,128)(2,1)S(1)} %copy-done.2, pred[3072]{0:T(1024)(128)(4,1)S(1)} %broadcast_compare_fusion.1, pred[768]{0:T(1024)(128)(4,1)S(1)} %broadcast_compare_fusion.3), kind=kOutput, calls=%fused_computation.18 | convolution fusion | flops 1219756032 | bytes 11407104 | tf_op jit(solution)/shard_map/dot_general | solution.py:102
  371.9 9.0 %gather_fusion.7 = bf16[512,3072]{1,0:T(8,128)(2,1)S(1)} fusion(bf16[768,3072]{1,0:T(8,128)(2,1)} %and_select_fusion, s32[1024]{0:T(1024)S(1)} %pad_clamp_fusion.1), kind=kCustom, calls=%fused_computation.7 | custom fusion | bytes 6293504 | tf_op jit(solution)/shard_map/gather | solution.py:31
  380.9 1.9 broadcast_select_fusion.3
  382.9 0.0 all-reduce.13.cloned.1.call-update
  382.9 0.3 all-reduce.15.cloned.1.call-start
  383.2 4.5 gather_fusion
  387.7 3.8 scatter_custom_fusion.5
  391.4 4.5 gather_fusion.8
  396.0 106.6 %all-reduce.13.cloned.1.call-done = bf16[512,3072]{1,0:T(8,128)(2,1)} async-done(((bf16[512,3072]{1,0:T(8,128)(2,1)}), bf16[512,3072]{1,0:T(8,128)(2,1)}) %all-reduce.13.cloned.1.call-update) | async-done | bytes 3145744 | tf_op jit(solution)/shard_map/psum | solution.py:82
  502.6 12.0 %gather_fusion.9 = bf16[768,3072]{1,0:T(8,128)(2,1)} fusion(bf16[512,3072]{1,0:T(8,128)(2,1)} %all-reduce.13.cloned.1.call-done, s32[1024]{0:T(1024)S(1)} %pad_clamp_fusion), kind=kCustom, calls=%fused_computation.9 | custom fusion | bytes 9440256 | tf_op jit(solution)/shard_map/gather | solution.py:42
  514.6 4.4 broadcast_select_fusion.1
  519.0 0.0 copy-start.1
  519.0 2.2 copy-done.1
  521.2 1.0 fusion.13
  522.2 0.0 all-reduce.15.cloned.1.call-update
  522.2 0.0 all-reduce.17.cloned.1.call-start
  522.3 0.0 copy-done.8
  522.3 3.1 fusion.3
  525.4 0.0 all-reduce.17.cloned.1.call-update
  525.5 65.2 %all-reduce.15.cloned.1.call-done = bf16[768,256]{1,0:T(8,128)(2,1)} async-done(((bf16[768,256]{1,0:T(8,128)(2,1)}), bf16[768,256]{1,0:T(8,128)(2,1)}) %all-reduce.15.cloned.1.call-update) | async-done | bytes 393232 | tf_op jit(solution)/shard_map/psum | solution.py:9
  590.7 2.9 fusion.19
  593.6 119.7 %all-reduce.17.cloned.1.call-done = bf16[256,3072]{1,0:T(8,128)(2,1)} async-done(((bf16[256,3072]{1,0:T(8,128)(2,1)}), bf16[256,3072]{1,0:T(8,128)(2,1)}) %all-reduce.17.cloned.1.call-update) | async-done | bytes 1572880 | tf_op jit(solution)/shard_map/psum | solution.py:9
  713.3 3.7 fusion.6
  717.0 0.0 copy-done.5
  717.0 0.0 copy-done.3
  717.0 7.8 %and_select_fusion.1 = bf16[768,3072]{1,0:T(8,128)(2,1)} fusion(bf16[768,3072]{1,0:T(8,128)(2,1)} %fusion.6, bf16[768,256]{1,0:T(8,128)(2,1)S(1)} %copy-done.5, bf16[256,3072]{1,0:T(8,128)(2,1)S(1)} %copy-done.3, pred[3072]{0:T(1024)(128)(4,1)S(1)} %broadcast_compare_fusion, pred[768]{0:T(1024)(128)(4,1)S(1)} %broadcast_compare_fusion.2), kind=kOutput, calls=%fused_computation.19 | convolution fusion | flops 1219756032 | bytes 11407104 | tf_op jit(solution)/shard_map/dot_general | solution.py:102
  (45 shorter events, 0.4 us)
Async XLA Ops:
  6.5 142.9 %all-reduce.7.cloned.1.call-start = ((), (), s32[]{:S(2)}) async-start(), calls=%async_computation | async-start | bytes 6291456 | tf_op jit(solution)/shard_map/psum | solution.py:82
  25.7 211.9 %all-reduce.9.cloned.1.call-start = ((), (), s32[]{:S(2)}) async-start(), calls=%async_computation.1 | async-start | bytes 786432 | tf_op jit(solution)/shard_map/psum | solution.py:9
  161.4 6.6 copy-start.6
  161.4 7.7 %copy-start.7 = (bf16[2,256,256]{2,1,0:T(8,128)(2,1)S(1)}, bf16[2,256,256]{2,1,0:T(8,128)(2,1)}, u32[]{:S(2)}) copy-start(bf16[2,256,256]{2,1,0:T(8,128)(2,1)} %param.14) | copy-start | bytes 786436
  165.8 2.2 copy-start
  169.0 191.3 %all-reduce.11.cloned.1.call-start = ((), (), s32[]{:S(2)}) async-start(), calls=%async_computation.2 | async-start | bytes 3145728 | tf_op jit(solution)/shard_map/psum | solution.py:9
  172.3 330.4 %all-reduce.13.cloned.1.call-start = ((), (), s32[]{:S(2)}) async-start(), calls=%async_computation.3 | async-start | bytes 6291456 | tf_op jit(solution)/shard_map/psum | solution.py:82
  237.5 126.5 %copy-start.4 = (bf16[768,256]{1,0:T(8,128)(2,1)S(1)}, bf16[768,256]{1,0:T(8,128)(2,1)}, u32[]{:S(2)}) copy-start(bf16[768,256]{1,0:T(8,128)(2,1)} %all-reduce.9.cloned.1.call-done) | copy-start | bytes 1179652
  360.3 3.7 copy-start.2
  382.9 207.8 %all-reduce.15.cloned.1.call-start = ((), (), s32[]{:S(2)}) async-start(), calls=%async_computation.4 | async-start | bytes 786432 | tf_op jit(solution)/shard_map/psum | solution.py:9
  514.6 7.7 %copy-start.8 = (bf16[2,256,256]{2,1,0:T(8,128)(2,1)S(1)}, bf16[2,256,256]{2,1,0:T(8,128)(2,1)}, u32[]{:S(2)}) copy-start(bf16[2,256,256]{2,1,0:T(8,128)(2,1)} %param.14) | copy-start | bytes 786436
  519.0 2.2 copy-start.1
  522.2 191.1 %all-reduce.17.cloned.1.call-start = ((), (), s32[]{:S(2)}) async-start(), calls=%async_computation.5 | async-start | bytes 3145728 | tf_op jit(solution)/shard_map/psum | solution.py:9
  590.7 126.3 %copy-start.5 = (bf16[768,256]{1,0:T(8,128)(2,1)S(1)}, bf16[768,256]{1,0:T(8,128)(2,1)}, u32[]{:S(2)}) copy-start(bf16[768,256]{1,0:T(8,128)(2,1)} %all-reduce.15.cloned.1.call-done) | copy-start | bytes 1179652
  713.3 3.7 copy-start.3
Sparse Core Ops, SparseCore 0:
  25.8 123.5 all-reduce.6
  169.1 68.3 all-reduce.8
  241.2 119.0 all-reduce.10
  383.0 119.5 all-reduce.12
  522.3 68.3 all-reduce.14
  594.2 119.0 all-reduce.16
where the time goes:
time: 732 us
  waiting for transfers between devices  580 us (79%)
  local copies, waits for them, and re-layouts  77.6 us (11%)
  other arithmetic  35.7 us (5%)
  matrix products  24 us (3%)
  between operations  13.9 us (2%)
    psum x4, waiting for transfers between devices, broadcast(): return lax.psum(jnp.where(mine, array, jnp.zeros_like(array)), axis)  370 us
    psum x2, waiting for transfers between devices, per_device(): received = lax.psum(picked, 'row').astype(jnp.float32).astype(jnp.bfloat16)  210 us
    gather x4, local copies, waits for them, and re-layouts, place_rows(): arriving = received[jnp.minimum(slot[glob_row], listed - 1)]  32.9 us
    gather x2, local copies, waits for them, and re-layouts, pick_rows(): chosen = matrix[local_index]  18.1 us
    dot_general x2, matrix products, per_device(): jnp.dot(lower_recv, upper_recv, preferred_element_type=jnp.float32)  15.7 us
  transfers between devices with their start and end apart: 6, of which 6 were waited for; matrix products, arithmetic and copies ran while one was open for 6% of the time, Pallas kernels for 0%

commit v1 on v0

v1 whole, which is shorter than its diff:
```python
import functools

import jax
import jax.numpy as jnp
from jax import lax
from jax.experimental import pallas as pl
from jax.experimental.pallas import tpu as pltpu
from jax.sharding import PartitionSpec as P

MESH = pl.DeviceIdType.MESH
NB = 256
SIDE = 4
ZS = 8
ROWS, COLS = 768, 3072
WIDE = COLS + 2 * NB
CHUNK = 768
BIG = SIDE * 16
SHARD = 16
BF = jnp.bfloat16
F32 = jnp.float32


def dot(a, b):
    return jnp.dot(a, b, preferred_element_type=F32)


def turned(row):
    n = row.shape[1]
    i = lax.broadcasted_iota(jnp.int32, (n, n), 0)
    j = lax.broadcasted_iota(jnp.int32, (n, n), 1)
    return jnp.sum(jnp.where(i == j, row, 0), axis=1, keepdims=True)


def kernel(
    a_hbm, piv_ref, li_hbm, ui_hbm, out_hbm,
    a, ap, t, s, ps, po, xr, r1, q, r2, ss, w, lo, d, oh, keep, l0t, x1t, li, ui,
    load_sem, store_sem,
    x_ss, x_rs, r1_ss, r1_rs, r2_ss, r2_rs, s1_ss, s1_rs, s2_ss, s2_rs,
    g1_ss, g1_rs, g2_ss, g2_rs, c_ss, c_rs, z_ss, z_rs, e_ss, e_rs,
):
    row = lax.axis_index("row")
    z = lax.axis_index("col")
    core = lax.rem(row, 2)
    yy = lax.rem(row // 2, SIDE)
    xx = row // (2 * SIDE)
    m = jnp.where(core == 0, xx, yy)
    n = jnp.where(core == 0, yy, xx)

    def at(mm, nn):
        mm, nn = lax.rem(mm + SIDE, SIDE), lax.rem(nn + SIDE, SIDE)
        return (jnp.where(core == 0, mm * SIDE + nn, nn * SIDE + mm) * 2 + core, z)

    sibling = (row + 1 - 2 * core, z)

    def along(k):
        return (row, lax.rem(z + k + ZS, ZS))

    sent = []

    def send(src, dst, ss_, rs_, dev):
        copy = pltpu.make_async_remote_copy(
            src_ref=src, dst_ref=dst, send_sem=ss_, recv_sem=rs_, device_id=dev, device_id_type=MESH
        )
        return copy

    load_a = pltpu.make_async_copy(a_hbm, a, load_sem.at[0])
    load_l = pltpu.make_async_copy(li_hbm, li, load_sem.at[1])
    load_u = pltpu.make_async_copy(ui_hbm, ui, load_sem.at[2])
    load_a.start()
    load_l.start()
    load_u.start()

    barrier = pltpu.get_barrier_semaphore()
    partners = [sibling]
    partners += [at(m + k, n) for k in (1, 2, 3)]
    partners += [at(m, n + k) for k in (1, 2, 3)]
    partners += [along(k) for k in range(1, ZS)]
    for dev in partners:
        pl.semaphore_signal(barrier, inc=1, device_id=dev, device_id_type=MESH)

    p0r, p1r = piv_ref[0:1, :], piv_ref[1:2, :]
    p0c, p1c = turned(p0r), turned(p1r)
    i0 = lax.broadcasted_iota(jnp.int32, (NB, NB), 0)
    i1 = lax.broadcasted_iota(jnp.int32, (NB, NB), 1)
    hit = p1c == p0r
    src1 = jnp.where(
        jnp.max(hit.astype(jnp.int32), axis=1, keepdims=True) > 0,
        jnp.sum(jnp.where(hit, i1, 0), axis=1, keepdims=True),
        p1c,
    )
    src0 = p0c
    inner = p0r == NB + i0
    out_in = jnp.sum(jnp.where(inner, p1c, 0), axis=0, keepdims=True)
    met = jnp.max(hit.astype(jnp.int32), axis=0, keepdims=True) > 0
    met_at = jnp.sum(jnp.where(hit, NB + i0, 0), axis=0, keepdims=True)
    dest0 = jnp.where(p0r < NB, p0r, jnp.where(p0r < 2 * NB, out_in, jnp.where(met, met_at, p0r)))
    back = p0c == NB + i1
    dest1 = jnp.where(
        jnp.max(back.astype(jnp.int32), axis=0, keepdims=True) > 0,
        jnp.sum(jnp.where(back, i0, 0), axis=0, keepdims=True),
        p1r,
    )
    for b in range(ROWS // NB):
        base = b * (NB * 2 * SIDE * SIDE) + row * NB
        rows = pl.ds(b * NB, NB)
        glob_c = base + i0
        glob_r = base + i1
        d0 = dest0 == glob_c
        d1 = dest1 == glob_c
        d[rows, 0:NB] = d0.astype(F32).astype(BF)
        d[rows, NB : 2 * NB] = d1.astype(F32).astype(BF)
        moved = jnp.max(jnp.maximum(d0.astype(F32), d1.astype(F32)), axis=1, keepdims=True)
        keep[rows, :] = jnp.broadcast_to(1.0 - moved, (NB, 128))
        oh[0:NB, b * NB : (b + 1) * NB] = (src0 == glob_r).astype(F32).astype(BF)
        oh[NB : 2 * NB, b * NB : (b + 1) * NB] = (src1 == glob_r).astype(F32).astype(BF)

    load_a.wait()
    pl.semaphore_wait(barrier, len(partners))

    mine = core * NB
    other = NB - mine

    def z_copy(blk, b, to, way, first):
        rows = pl.ds(b * NB, NB)
        cols = pl.ds(blk * NB, NB)
        src = a.at[rows, pl.ds(0, NB)] if first else w.at[rows, cols]
        return send(src, w.at[rows, cols], z_ss.at[blk, b, way], z_rs.at[blk, b], along(to))

    def z_start(blk):
        @pl.when(z == blk)
        def _():
            for b in range(ROWS // NB):
                z_copy(blk, b, 1, 0, True).start()
                z_copy(blk, b, -1, 1, True).start()
            w[:, blk * NB : (blk + 1) * NB] = a[:, 0:NB]

    def z_pass(blk, b):
        rel = lax.rem(z - blk + ZS, ZS)

        @pl.when(rel != 0)
        def _():
            z_copy(blk, b, 1, 0, False).wait_recv()

        @pl.when((rel >= 1) & (rel <= 3))
        def _():
            z_copy(blk, b, 1, 0, False).start()

        @pl.when(rel >= 6)
        def _():
            z_copy(blk, b, -1, 1, False).start()

    def z_end(blk):
        rel = lax.rem(z - blk + ZS, ZS)
        for b in range(ROWS // NB):

            @pl.when(rel <= 3)
            def _():
                z_copy(blk, b, 1, 0, False).wait_send()

            @pl.when((rel == 0) | (rel >= 6))
            def _():
                z_copy(blk, b, -1, 1, False).wait_send()

    root = (m == 0) & (n == 0)

    def s1_copy(k):
        return send(a.at[pl.ds(k * BIG, BIG)], ss, s1_ss.at[k - 1], s1_rs, at(k, 0))

    def s_start():
        @pl.when(root)
        def _():
            for k in (1, 3, 2):
                s1_copy(k).start()
            ss[...] = a[0:BIG, :]

    def shard(mm, nn):
        return pl.ds(pl.multiple_of(mine + mm * BIG + nn * SHARD, SHARD), SHARD)

    def s2_copy(k):
        return send(
            ss.at[pl.ds(k * SHARD, SHARD)], s.at[shard(m, k), pl.ds(0, COLS)],
            s2_ss.at[k - 1], s2_rs, at(m, k),
        )

    def s_second():
        @pl.when((n == 0) & (m != 0))
        def _():
            s1_copy(1).wait_recv()

        @pl.when(n == 0)
        def _():
            for k in (1, 3, 2):
                s2_copy(k).start()
            s[shard(m, 0), 0:COLS] = ss[0:SHARD, :]

    def s_third():
        @pl.when(n != 0)
        def _():
            s2_copy(1).wait_recv()

    def s_end():
        @pl.when(root)
        def _():
            for k in (1, 3, 2):
                s1_copy(k).wait_send()

        @pl.when(n == 0)
        def _():
            for k in (1, 3, 2):
                s2_copy(k).wait_send()

    bufs = (t, s)

    def e_copy(kind, blk, k):
        buf = bufs[kind]
        rows = shard(m, n)
        return send(
            buf.at[rows, pl.ds(0, NB)], buf.at[rows, pl.ds(COLS + blk * NB, NB)],
            e_ss.at[kind, k - 1], e_rs.at[kind, blk], along(k),
        )

    def e_start(kind):
        for blk in range(2):

            @pl.when(z == blk)
            def _():
                for k in (4, 3, 5, 2, 6, 1, 7):
                    e_copy(kind, blk, k).start()
                bufs[kind][shard(m, n), COLS + blk * NB : COLS + (blk + 1) * NB] = bufs[kind][shard(m, n), 0:NB]

    def e_recv(kind):
        for blk in range(2):

            @pl.when(z != blk)
            def _():
                e_copy(kind, blk, 1).wait_recv()

    def e_end(kind):
        @pl.when(z < 2)
        def _():
            for k in range(1, ZS):
                e_copy(kind, 0, k).wait_send()

    def cols_of(c):
        return pl.ds(c * CHUNK, CHUNK)

    def x_copy(c):
        return send(ps.at[:, cols_of(c)], xr.at[:, cols_of(c)], x_ss.at[c], x_rs.at[c], sibling)

    def picks(c):
        def tile(half, into):
            def body(i, carry):
                cc = pl.ds(pl.multiple_of(c * CHUNK + i * NB, NB), NB)
                into[:, cc] = dot(oh[pl.ds(pl.multiple_of(half, NB), NB), :], a[:, cc]).astype(BF)
                return carry

            lax.fori_loop(0, CHUNK // NB, body, 0)

        tile(other, ps)
        x_copy(c).start()
        tile(mine, po)

    def r1_copy(c, k):
        g = lax.rem(m + k, SIDE)
        return send(
            po.at[pl.ds(pl.multiple_of(g * BIG, BIG), BIG), cols_of(c)], r1.at[k - 1, :, cols_of(c)],
            r1_ss.at[c, k - 1], r1_rs.at[c, k - 1], at(m + k, n),
        )

    def reduce_core(c):
        x_copy(c).wait_recv()
        po[:, cols_of(c)] = po[:, cols_of(c)] + xr[:, cols_of(c)]
        for k in (2, 1, 3):
            r1_copy(c, k).start()

    def r2_copy(c, k):
        g = lax.rem(n + k, SIDE)
        return send(
            q.at[pl.ds(pl.multiple_of(g * SHARD, SHARD), SHARD), cols_of(c)], r2.at[k - 1, :, cols_of(c)],
            r2_ss.at[c, k - 1], r2_rs.at[c, k - 1], at(m, n + k),
        )

    def reduce_major(c):
        for k in (1, 3, 2):
            r1_copy(c, k).wait_recv()
        cc = cols_of(c)
        own = po[pl.ds(pl.multiple_of(m * BIG, BIG), BIG), cc]
        q[:, cc] = (own + r1[0, :, cc]) + (r1[1, :, cc] + r1[2, :, cc])
        for k in (2, 1, 3):
            r2_copy(c, k).start()

    def reduce_minor(c):
        for k in (1, 3, 2):
            r2_copy(c, k).wait_recv()
        cc = cols_of(c)
        own = q[pl.ds(pl.multiple_of(n * SHARD, SHARD), SHARD), cc]
        t[shard(m, n), cc] = (own + r2[0, :, cc]) + (r2[1, :, cc] + r2[2, :, cc])

    items = [(1, 0, COLS // 2), (1, COLS // 2, COLS // 2), (1, COLS, 2 * NB), (0, COLS, 2 * NB)]
    first_t = len(items)
    items += [(0, c * CHUNK, CHUNK) for c in range(COLS // CHUNK)]

    def g1_copy(i, k):
        kind, c0, width = items[i]
        part = bufs[kind].at[shard(m, n), pl.ds(c0, width)]
        return send(part, part, g1_ss.at[i, k - 1], g1_rs.at[i, k - 1], at(m, n + k))

    def gather_minor(i):
        for k in (2, 1, 3):
            g1_copy(i, k).start()

    def block(mm):
        return pl.ds(pl.multiple_of(mine + lax.rem(mm + SIDE, SIDE) * BIG, BIG), BIG)

    ways = ((0, 0, 1), (0, 1, -1), (0, 1, 1), (0, 0, -1), (-1, 0, 1), (1, 1, -1))

    def g2_copy(i, j):
        kind, c0, width = items[i]
        who, half, way = ways[j]
        part = bufs[kind].at[block(m + who), pl.ds(c0 + half * (width // 2), width // 2)]
        return send(part, part, g2_ss.at[i, j], g2_rs.at[i, j], at(m + way, n))

    def gather_major(i):
        for k in (1, 3, 2):
            g1_copy(i, k).wait_recv()
        for j in range(4):
            g2_copy(i, j).start()

    def gather_pass(i):
        g2_copy(i, 0).wait_recv()
        g2_copy(i, 4).start()
        g2_copy(i, 1).wait_recv()
        g2_copy(i, 5).start()

    def c_copy(i):
        kind, c0, width = items[i]
        part = bufs[kind].at[pl.ds(pl.multiple_of(mine, NB), NB), pl.ds(c0, width)]
        return send(part, part, c_ss.at[i], c_rs.at[i], sibling)

    def gather_core(i):
        for j in (2, 3, 4, 5):
            g2_copy(i, j).wait_recv()
        c_copy(i).start()

    def gathered(i):
        c_copy(i).wait_recv()

    def displaced(c0, width):
        def body(i, carry):
            cc = pl.ds(pl.multiple_of(c0 + i * NB, NB), NB)
            for b in range(ROWS // NB):
                rows = pl.ds(b * NB, NB)
                stay = jnp.concatenate([keep[rows, :], keep[rows, :]], axis=1) > 0.5
                arriving = dot(d[rows, :], s[:, cc])
                ap[rows, cc] = jnp.where(stay, a[rows, cc].astype(F32), arriving).astype(BF)
            return carry

        lax.fori_loop(0, width // NB, body, 0)

    def lowers():
        l0t[...] = dot(t[NB : 2 * NB, COLS : COLS + NB], ui[0]).astype(BF)
        u0w = dot(li[0], t[0:NB, COLS + NB : WIDE]).astype(BF)
        x1t[...] = (t[NB : 2 * NB, COLS + NB : WIDE].astype(F32) - dot(l0t[...], u0w)).astype(BF)

        def body(b, carry):
            rows = pl.ds(pl.multiple_of(b * NB, NB), NB)
            stay = jnp.concatenate([keep[rows, :], keep[rows, :]], axis=1) > 0.5
            w0 = jnp.where(stay, w[rows, 0:NB].astype(F32), dot(d[rows, :], s[:, COLS : COLS + NB])).astype(BF)
            w1 = jnp.where(stay, w[rows, NB : 2 * NB].astype(F32), dot(d[rows, :], s[:, COLS + NB : WIDE]))
            low0 = dot(w0, ui[0]).astype(BF)
            x1 = (w1 - dot(low0, u0w)).astype(BF)
            lo[rows, 0:NB] = low0
            lo[rows, NB : 2 * NB] = dot(x1, ui[1]).astype(BF)
            return carry

        lax.fori_loop(0, ROWS // NB, body, 0)

    def update(c):
        def body(i, carry):
            cc = pl.ds(pl.multiple_of(c * CHUNK + i * NB, NB), NB)
            u0 = dot(li[0], t[0:NB, cc]).astype(BF)
            x1 = (t[NB : 2 * NB, cc].astype(F32) - dot(l0t[...], u0)).astype(BF)
            u1 = dot(li[1], x1).astype(BF)
            uu = jnp.concatenate([u0, u1], axis=0)
            ap[:, cc] = (ap[:, cc].astype(F32) - dot(lo[...], uu)).astype(BF)

            @pl.when(row == 0)
            def _():
                ap[0:NB, cc] = u0

            @pl.when(row == 1)
            def _():
                ap[0:NB, cc] = u1

            return carry

        lax.fori_loop(0, CHUNK // NB, body, 0)
        if c == 0:

            @pl.when((z == 0) & (row > 0))
            def _():
                ap[0:NB, 0:NB] = lo[0:NB, 0:NB]

            @pl.when((z == 1) & (row > 1))
            def _():
                ap[0:NB, 0:NB] = lo[0:NB, NB : 2 * NB]

            @pl.when(z == 0)
            def _():
                ap[NB:ROWS, 0:NB] = lo[NB:ROWS, 0:NB]

            @pl.when(z == 1)
            def _():
                ap[NB:ROWS, 0:NB] = lo[NB:ROWS, NB : 2 * NB]

            @pl.when((z == 0) & (row == 0))
            def _():
                ap[0:NB, 0:NB] = t[0:NB, 0:NB]

            @pl.when((z == 0) & (row == 1))
            def _():
                ap[0:NB, 0:NB] = l0t[...]

            @pl.when((z == 1) & (row == 1))
            def _():
                ap[0:NB, 0:NB] = x1t[...]

    def store(c):
        return pltpu.make_async_copy(ap.at[:, cols_of(c)], out_hbm.at[:, cols_of(c)], store_sem.at[c])

    chunks = COLS // CHUNK
    s_start()
    z_start(0)
    z_start(1)
    picks(0)
    for c in range(1, chunks):
        picks(c)
        reduce_core(c - 1)
    reduce_core(chunks - 1)
    for b in range(ROWS // NB):
        z_pass(1, b)
        z_pass(0, b)
    reduce_major(0)
    s_second()
    reduce_major(1)
    reduce_minor(0)
    e_start(0)
    s_third()
    e_start(1)
    gather_minor(0)
    gather_minor(1)
    reduce_major(2)
    reduce_minor(1)
    e_recv(1)
    gather_minor(2)
    e_recv(0)
    gather_minor(3)
    gather_minor(4)
    gather_major(0)
    reduce_major(3)
    gather_minor(5)
    gather_major(1)
    reduce_minor(2)
    gather_minor(6)
    gather_pass(0)
    reduce_minor(3)
    gather_minor(7)
    gather_major(2)
    gather_major(3)
    gather_pass(1)
    gather_major(4)
    gather_pass(2)
    gather_pass(3)
    gather_core(0)
    gather_major(5)
    gather_core(1)
    gather_pass(4)
    gather_core(2)
    gather_core(3)
    gather_major(6)
    gathered(0)
    displaced(0, COLS // 2)
    gather_pass(5)
    gather_core(4)
    gather_major(7)
    gathered(1)
    displaced(COLS // 2, COLS // 2)
    gather_pass(6)
    gather_core(5)
    gathered(2)
    gathered(3)
    load_l.wait()
    load_u.wait()
    lowers()
    gather_pass(7)
    gather_core(6)
    gathered(4)
    update(0)
    store(0).start()
    gathered(5)
    update(1)
    store(1).start()
    gather_core(7)
    gathered(6)
    update(2)
    store(2).start()
    gathered(7)
    update(3)
    store(3).start()

    s_end()
    z_end(0)
    z_end(1)
    e_end(0)
    e_end(1)
    for c in range(chunks):
        x_copy(c).wait_send()
        for k in (1, 2, 3):
            r1_copy(c, k).wait_send()
            r2_copy(c, k).wait_send()
    for i in range(len(items)):
        for k in (1, 2, 3):
            g1_copy(i, k).wait_send()
        for j in range(6):
            g2_copy(i, j).wait_send()
        c_copy(i).wait_send()
    for c in range(chunks):
        store(c).wait()


def per_device(a_stored, pivots, l_inverse, u_inverse):
    chunks = COLS // CHUNK
    n_items = 4 + chunks
    dma = pltpu.SemaphoreType.DMA
    anyspace = pl.BlockSpec(memory_space=pl.ANY)
    scratch = [
        pltpu.VMEM((ROWS, COLS), BF),
        pltpu.VMEM((ROWS, COLS), BF),
        pltpu.VMEM((2 * NB, WIDE), BF),
        pltpu.VMEM((2 * NB, WIDE), BF),
        pltpu.VMEM((NB, COLS), BF),
        pltpu.VMEM((NB, COLS), BF),
        pltpu.VMEM((NB, COLS), BF),
        pltpu.VMEM((3, BIG, COLS), BF),
        pltpu.VMEM((BIG, COLS), BF),
        pltpu.VMEM((3, SHARD, COLS), BF),
        pltpu.VMEM((BIG, COLS), BF),
        pltpu.VMEM((ROWS, 2 * NB), BF),
        pltpu.VMEM((ROWS, 2 * NB), BF),
        pltpu.VMEM((ROWS, 2 * NB), BF),
        pltpu.VMEM((2 * NB, ROWS), BF),
        pltpu.VMEM((ROWS, 128), F32),
        pltpu.VMEM((NB, NB), BF),
        pltpu.VMEM((NB, NB), BF),
        pltpu.VMEM((2, NB, NB), BF),
        pltpu.VMEM((2, NB, NB), BF),
        dma((3,)), dma((chunks,)),
        dma((chunks,)), dma((chunks,)),
        dma((chunks, 3)), dma((chunks, 3)),
        dma((chunks, 3)), dma((chunks, 3)),
        dma((3,)), dma,
        dma((3,)), dma,
        dma((n_items, 3)), dma((n_items, 3)),
        dma((n_items, 6)), dma((n_items, 6)),
        dma((n_items,)), dma((n_items,)),
        dma((2, 3, 2)), dma((2, 3)),
        dma((2, ZS - 1)), dma((2, 2)),
    ]
    return pl.pallas_call(
        kernel,
        out_shape=jax.ShapeDtypeStruct((ROWS, COLS), BF),
        in_specs=[anyspace, pl.BlockSpec(memory_space=pltpu.VMEM), anyspace, anyspace],
        out_specs=anyspace,
        scratch_shapes=scratch,
        compiler_params=pltpu.CompilerParams(
            collective_id=0, has_side_effects=True, vmem_limit_bytes=48 * 2**20
        ),
        name="panels",
    )(a_stored, pivots, l_inverse, u_inverse)


def solution(mesh):
    in_specs = (P("row", "col"), P(), P(), P())
    out_specs = P("row", "col")
    return jax.shard_map(
        per_device, mesh=mesh, in_specs=in_specs, out_specs=out_specs, check_vma=False
    )
```

time: 732 us -> 94.8 us (0.13)
  the two profiles are of different devices: /device:TPU:1 before, /device:TPU:160 now
where the time goes in v1:
time: 94.8 us; the launch traced here: 94.6 us
  Pallas kernels  89.9 us (95%)
  local copies, waits for them, and re-layouts  4.77 us (5%)
    pallas_call x1, Pallas kernels, per_device(): pl.pallas_call(kernel, out_shape=jax.ShapeDtypeStruct((ROWS, COLS), BF),...  89.9 us
    unnamed x7, local copies, waits for them, and re-layouts  4.77 us

profile of v1, /device:TPU:160, one launch (start us, length us, event | category | flops | bytes accessed | tf_op | source)
XLA Modules:
  0.0 94.6 jit_solution(6168570147702507214)
XLA Ops:
  0.0 0.0 copy-start
  0.0 0.9 %copy-done = bf16[2,256,256]{2,1,0:T(8,128)(2,1)S(1)} copy-done((bf16[2,256,256]{2,1,0:T(8,128)(2,1)S(1)}, bf16[2,256,256]{2,1,0:T(8,128)(2,1)}, u32[]{:S(2)}) %copy-start) | copy-done | bytes 262168
  1.0 0.0 copy-start.1
  1.0 0.9 %copy-done.1 = bf16[2,256,256]{2,1,0:T(8,128)(2,1)S(1)} copy-done((bf16[2,256,256]{2,1,0:T(8,128)(2,1)S(1)}, bf16[2,256,256]{2,1,0:T(8,128)(2,1)}, u32[]{:S(2)}) %copy-start.1) | copy-done | bytes 262168
  1.9 0.0 copy-start.2
  1.9 0.7 copy-done.2
  2.6 89.9 %panels.1 = bf16[768,3072]{1,0:T(8,128)(2,1)S(1)} custom-call(bf16[768,3072]{1,0:T(8,128)(2,1)} %a_hbm.1, s32[2,256]{1,0:T(2,128)S(1)} %copy-done.2, bf16[2,256,256]{2,1,0:T(8,128)(2,1)S(1)} %copy-done, bf16[2,256,256]{2,1,0:T(8,128)(2,1)S(1)} %copy-done.1), custom_call_target="tpu_custom_call" | custom-call | tf_op jit(solution)/shard_map/panels/pallas_call | solution.py:569
  92.4 2.2 %copy.6 = bf16[768,3072]{1,0:T(8,128)(2,1)} copy(bf16[768,3072]{1,0:T(8,128)(2,1)S(1)} %panels.1) | data formatting | bytes 9437184
Async XLA Ops:
  0.0 0.9 %copy-start = (bf16[2,256,256]{2,1,0:T(8,128)(2,1)S(1)}, bf16[2,256,256]{2,1,0:T(8,128)(2,1)}, u32[]{:S(2)}) copy-start(bf16[2,256,256]{2,1,0:T(8,128)(2,1)} %li_hbm.1) | copy-start | bytes 786436
  1.0 0.9 %copy-start.1 = (bf16[2,256,256]{2,1,0:T(8,128)(2,1)S(1)}, bf16[2,256,256]{2,1,0:T(8,128)(2,1)}, u32[]{:S(2)}) copy-start(bf16[2,256,256]{2,1,0:T(8,128)(2,1)} %ui_hbm.1) | copy-start | bytes 786436
  1.9 0.7 copy-start.2

commit v2 on v1

v2 whole, which is shorter than its diff:
```python
import functools

import jax
import jax.numpy as jnp
from jax import lax
from jax.experimental import pallas as pl
from jax.experimental.pallas import tpu as pltpu
from jax.sharding import PartitionSpec as P

MESH = pl.DeviceIdType.MESH
NB = 256
SIDE = 4
ZS = 8
ROWS, COLS = 768, 3072
WIDTHS = (768, 768, 768, 768)
STARTS = tuple(sum(WIDTHS[:c]) for c in range(len(WIDTHS)))
CHUNKS = range(len(WIDTHS))
S_WIDTHS = (256, 768, 768, 768, 512)
S_STARTS = tuple(sum(S_WIDTHS[:c]) for c in range(len(S_WIDTHS)))
S_CHUNKS = range(len(S_WIDTHS))
TREE = (
    (1, 0, 0, 1), (1, 1, 1, 2), (1, 3, 3, 2), (2, 0, 0, 2), (0, 1, 2, 3), (0, 3, 2, 3), (1, 2, 3, 3), (2, 1, 1, 3),
    (2, 3, 0, 3), (3, 0, 0, 3), (0, 2, 2, 4), (2, 2, 1, 4), (3, 1, 0, 4), (3, 3, 0, 4), (3, 2, 0, 5),
)
DEPTH = 5
STEP_X, STEP_Y = (1, 0, -1, 0), (0, 1, 0, -1)
HALF = NB // 2
PLAN = (
    "v1", "picks0", "picks1", "v2", "core0", "z1", "core1", "picks2", "v3", "picks3", "places", "major0", "core2",
    "z2", "major1", "minor0", "n.T0", "et", "v4", "core3", "z3", "major2", "ert", "n.TE", "m.T0", "v5", "minor1",
    "es", "n.T1", "m.TE", "p.T0", "major3", "z4", "c.S0", "ers", "n.SE", "minor2", "n.T2", "p.TE", "m.T1", "c.T0",
    "v6", "minor3", "m.SE", "c.TE", "p.T1", "n.T3", "z5", "g.TE", "g.T0", "lowtop", "p.SE", "m.T2", "c.S1", "c.T1",
    "v7", "c.S2", "m.T3", "uppers0", "c.SE", "p.T2", "g.T1", "uppers1", "z6", "g.S0", "p.T3", "g.S1", "g.S2",
    "g.SE", "lowers", "c.T2", "v8", "update0", "update1", "g.T2", "c.T3", "uppers2", "c.S3", "v9", "c.S4",
    "update2", "g.T3", "uppers3", "g.S3", "update3", "g.S4", "update4",
)
BIG = SIDE * 16
SHARD = 16
BF = jnp.bfloat16
F32 = jnp.float32


def dot(a, b):
    return jnp.dot(a, b, preferred_element_type=F32)


def turned(row):
    n = row.shape[1]
    i = lax.broadcasted_iota(jnp.int32, (n, n), 0)
    j = lax.broadcasted_iota(jnp.int32, (n, n), 1)
    return jnp.sum(jnp.where(i == j, row, 0), axis=1, keepdims=True)


def kernel(
    a_hbm, piv_hbm, li_hbm, ui_hbm, ap,
    a, t, su, ps, po, xr, r1, q, r2, w, dl, oh, keep, l0t, u0w, li, ui, piv_ref,
    load_sem, part_sem,
    x_ss, x_rs, r1_ss, r1_rs, r2_ss, r2_rs, v_ss, v_rs,
    g1_ss, g1_rs, g2_ss, g2_rs, c_ss, c_rs, z_ss, z_rs, e_ss, e_rs,
):
    row = lax.axis_index("row")
    z = lax.axis_index("col")
    core = lax.rem(row, 2)
    yy = lax.rem(row // 2, SIDE)
    xx = row // (2 * SIDE)
    m = jnp.where(core == 0, xx, yy)
    n = jnp.where(core == 0, yy, xx)

    def at(mm, nn):
        mm, nn = lax.rem(mm + SIDE, SIDE), lax.rem(nn + SIDE, SIDE)
        return (jnp.where(core == 0, mm * SIDE + nn, nn * SIDE + mm) * 2 + core, z)

    sibling = (row + 1 - 2 * core, z)

    def along(k):
        return (row, lax.rem(z + k + ZS, ZS))

    s = su.at[pl.ds(0, 2 * NB)]

    def send(src, dst, ss_, rs_, dev):
        return pltpu.make_async_remote_copy(
            src_ref=src, dst_ref=dst, send_sem=ss_, recv_sem=rs_, device_id=dev, device_id_type=MESH
        )

    def load_a(c):
        cc = pl.ds(STARTS[c], WIDTHS[c])
        return pltpu.make_async_copy(a_hbm.at[:, cc], a.at[:, cc], part_sem.at[c])

    load_l = pltpu.make_async_copy(li_hbm, li, load_sem.at[1])
    load_u = pltpu.make_async_copy(ui_hbm, ui, load_sem.at[2])
    load_p = pltpu.make_async_copy(piv_hbm, piv_ref, load_sem.at[3])
    load_p.start()
    for c in CHUNKS:
        load_a(c).start()
    load_l.start()
    load_u.start()

    barrier = pltpu.get_barrier_semaphore()
    partners = [sibling]
    partners += [at(m + k, n) for k in (1, 2, 3)]
    partners += [at(m, n + k) for k in (1, 2, 3)]
    partners += [along(k) for k in range(1, ZS)]
    for dev in partners:
        pl.semaphore_signal(barrier, inc=1, device_id=dev, device_id_type=MESH)

    pl.semaphore_wait(barrier, len(partners))

    mine = core * NB

    def z_copy(blk, b, to, way, first):
        rows = pl.ds(b * NB, NB)
        cols = pl.ds(blk * NB, NB)
        src = a_hbm.at[rows, pl.ds(0, NB)] if first else w.at[rows, cols]
        return send(src, w.at[rows, cols], z_ss.at[blk, b, way], z_rs.at[blk, b], along(to))

    def own_panel(blk):
        return pltpu.make_async_copy(a_hbm.at[:, pl.ds(0, NB)], w.at[:, pl.ds(blk * NB, NB)], load_sem.at[4])

    def z_start(blk):
        @pl.when(z == blk)
        def _():
            for b in range(ROWS // NB):
                z_copy(blk, b, 1, 0, True).start()
                z_copy(blk, b, -1, 1, True).start()
            own_panel(blk).start()

    def z_wave(wave):
        for blk in (1, 0):
            rel = lax.rem(z - blk + ZS, ZS)
            for b in range(ROWS // NB):
                hops = wave - b
                if 1 <= hops <= 4:

                    @pl.when(rel == hops)
                    def _():
                        z_copy(blk, b, 1, 0, False).wait_recv()
                        if hops < 4:
                            z_copy(blk, b, 1, 0, False).start()

                if 1 <= hops <= 3:

                    @pl.when(rel == ZS - hops)
                    def _():
                        z_copy(blk, b, 1, 0, False).wait_recv()
                        if hops < 3:
                            z_copy(blk, b, -1, 1, False).start()

    def z_end(blk):
        rel = lax.rem(z - blk + ZS, ZS)

        for b in range(ROWS // NB):

            @pl.when(rel <= 3)
            def _():
                z_copy(blk, b, 1, 0, False).wait_send()

            @pl.when((rel == 0) | (rel >= 6))
            def _():
                z_copy(blk, b, -1, 1, False).wait_send()

    root = (m == 0) & (n == 0)

    def shard(mm, nn):
        return pl.ds(pl.multiple_of(mine + mm * BIG + nn * SHARD, SHARD), SHARD)

    own_rows = pltpu.make_async_copy(
        a_hbm.at[pl.ds(0, NB)], su.at[pl.ds(pl.multiple_of(mine, NB), NB), pl.ds(0, COLS)], load_sem.at[5]
    )
    flip = 1 - 2 * core

    depths, passes = [], []
    for sign in (1, -1):
        px = lax.rem(sign * m + SIDE, SIDE)
        py = lax.rem(sign * flip * n + SIDE, SIDE)
        depth = 0
        go = [False] * 4
        for x, y, way, h in TREE:
            depth = depth + jnp.where((px == x) & (py == y), h, 0)
            go[way] = go[way] | ((px == (x - STEP_X[way]) % SIDE) & (py == (y - STEP_Y[way]) % SIDE))
        depths.append(depth)
        passes.append(go)

    def v_copy(tree, b, way, first=False):
        sign = 1 - 2 * tree
        cols = pl.ds(S_STARTS[b], S_WIDTHS[b])
        dst = su.at[pl.ds(pl.multiple_of(mine + tree * HALF, HALF), HALF), cols]
        src = a_hbm.at[pl.ds(tree * HALF, HALF), cols] if first else dst
        to = at(m + sign * STEP_X[way], n + sign * flip * STEP_Y[way])
        return send(src, dst, v_ss.at[tree, b, way], v_rs.at[tree, b], to)

    def s_start():
        @pl.when(root)
        def _():
            own_rows.start()
            for b in S_CHUNKS:
                for tree in range(2):
                    v_copy(tree, b, 0, True).start()

    def s_wave(wave):
        for b in S_CHUNKS:
            hops = wave - b
            if not 1 <= hops <= DEPTH:
                continue
            for tree in range(2):

                @pl.when(depths[tree] == hops)
                def _():
                    v_copy(tree, b, 0).wait_recv()
                    for way in range(4):
                        if any(h == hops + 1 and e == way for _, _, e, h in TREE):

                            @pl.when(passes[tree][way])
                            def _():
                                v_copy(tree, b, way).start()

        if wave == 1:

            @pl.when(root)
            def _():
                own_rows.wait()

    def s_end():
        for tree in range(2):
            for b in S_CHUNKS:
                for way in range(4):

                    @pl.when(passes[tree][way])
                    def _():
                        v_copy(tree, b, way).wait_send()

    bufs = (t, s)

    def e_copy(kind, blk, k):
        rows = shard(m, n)
        buf = bufs[kind]
        to = COLS + blk * NB if kind else COLS
        return send(
            buf.at[rows, pl.ds(0, NB)], buf.at[rows, pl.ds(to, NB)], e_ss.at[kind, k - 1], e_rs.at[kind, blk], along(k)
        )

    def e_sources(kind):
        return ((0, z == 0), (1, z == 1)) if kind else ((0, z == 1 - core),)

    def e_start(kind):
        for blk, here in e_sources(kind):

            @pl.when(here)
            def _():
                for k in (4, 3, 5, 2, 6, 1, 7):
                    e_copy(kind, blk, k).start()
                to = COLS + blk * NB if kind else COLS
                bufs[kind][shard(m, n), to : to + NB] = bufs[kind][shard(m, n), 0:NB]

    def e_recv(kind):
        for blk, here in e_sources(kind):

            @pl.when(jnp.logical_not(here))
            def _():
                e_copy(kind, blk, 1).wait_recv()

    def e_end(kind):
        for blk, here in e_sources(kind):

            @pl.when(here)
            def _():
                for k in range(1, ZS):
                    e_copy(kind, blk, k).wait_send()

    def cols_of(c):
        return pl.ds(STARTS[c], WIDTHS[c])

    def x_copy(c):
        return send(ps.at[:, cols_of(c)], xr.at[:, cols_of(c)], x_ss.at[c], x_rs.at[c], sibling)

    def picks(c):
        load_a(c).wait()

        def body(i, carry):
            cc = pl.ds(pl.multiple_of(STARTS[c] + i * NB, NB), NB)
            both = dot(oh[...], a[:, cc]).astype(BF)
            ps[:, cc] = both[0:NB]
            po[:, cc] = both[NB : 2 * NB]
            return carry

        lax.fori_loop(0, WIDTHS[c] // NB, body, 0)
        x_copy(c).start()

    def r1_copy(c, k):
        g = lax.rem(m + k, SIDE)
        return send(
            po.at[pl.ds(pl.multiple_of(g * BIG, BIG), BIG), cols_of(c)], r1.at[k - 1, :, cols_of(c)],
            r1_ss.at[c, k - 1], r1_rs.at[c, k - 1], at(m + k, n),
        )

    def reduce_core(c):
        x_copy(c).wait_recv()
        po[:, cols_of(c)] = po[:, cols_of(c)] + xr[:, cols_of(c)]
        for k in (2, 1, 3):
            r1_copy(c, k).start()

    def r2_copy(c, k):
        g = lax.rem(n + k, SIDE)
        return send(
            q.at[pl.ds(pl.multiple_of(g * SHARD, SHARD), SHARD), cols_of(c)], r2.at[k - 1, :, cols_of(c)],
            r2_ss.at[c, k - 1], r2_rs.at[c, k - 1], at(m, n + k),
        )

    def reduce_major(c):
        for k in (1, 3, 2):
            r1_copy(c, k).wait_recv()
        cc = cols_of(c)
        own = po[pl.ds(pl.multiple_of(m * BIG, BIG), BIG), cc]
        q[:, cc] = (own + r1[0, :, cc]) + (r1[1, :, cc] + r1[2, :, cc])
        for k in (2, 1, 3):
            r2_copy(c, k).start()

    def reduce_minor(c):
        for k in (1, 3, 2):
            r2_copy(c, k).wait_recv()
        cc = cols_of(c)
        own = q[pl.ds(pl.multiple_of(n * SHARD, SHARD), SHARD), cc]
        t[shard(m, n), cc] = (own + r2[0, :, cc]) + (r2[1, :, cc] + r2[2, :, cc])

    items = [(1, S_STARTS[c], S_WIDTHS[c]) for c in S_CHUNKS] + [(1, COLS, 2 * NB), (0, COLS, NB)]
    items += [(0, STARTS[c], WIDTHS[c]) for c in CHUNKS]

    def g1_copy(i, k):
        kind, c0, width = items[i]
        part = bufs[kind].at[shard(m, n), pl.ds(c0, width)]
        return send(part, part, g1_ss.at[i, k - 1], g1_rs.at[i, k - 1], at(m, n + k))

    def gather_minor(i):
        for k in (2, 1, 3):
            g1_copy(i, k).start()

    def block(mm):
        return pl.ds(pl.multiple_of(mine + lax.rem(mm + SIDE, SIDE) * BIG, BIG), BIG)

    ways = ((0, 0, 1), (0, 1, -1), (0, 1, 1), (0, 0, -1), (-1, 0, 1), (1, 1, -1))

    def g2_copy(i, j):
        kind, c0, width = items[i]
        who, half, way = ways[j]
        part = bufs[kind].at[block(m + who), pl.ds(c0 + half * (width // 2), width // 2)]
        return send(part, part, g2_ss.at[i, j], g2_rs.at[i, j], at(m + way, n))

    def gather_major(i):
        for k in (1, 3, 2):
            g1_copy(i, k).wait_recv()
        for j in range(4):
            g2_copy(i, j).start()

    def gather_pass(i):
        g2_copy(i, 0).wait_recv()
        g2_copy(i, 4).start()
        g2_copy(i, 1).wait_recv()
        g2_copy(i, 5).start()

    def c_copy(i):
        kind, c0, width = items[i]
        part = bufs[kind].at[pl.ds(pl.multiple_of(mine, NB), NB), pl.ds(c0, width)]
        return send(part, part, c_ss.at[i], c_rs.at[i], sibling)

    def gather_core(i):
        if i >= len(S_WIDTHS):
            for j in (2, 3, 4, 5):
                g2_copy(i, j).wait_recv()
        c_copy(i).start()

    def gathered(i):
        c_copy(i).wait_recv()

    def lowtop():
        load_l.wait()
        load_u.wait()
        l0t[...] = dot(t[NB : 2 * NB, COLS : COLS + NB], ui[0]).astype(BF)
        u0w[...] = dot(li[0], t[0:NB, COLS : COLS + NB]).astype(BF)

    def lowers():
        for blk in range(2):

            @pl.when(z == blk)
            def _():
                own_panel(blk).wait()

        def body(b, carry):
            rows = pl.ds(pl.multiple_of(b * NB, NB), NB)
            stay = jnp.concatenate([keep[rows, :], keep[rows, :]], axis=1) > 0.5
            take = dl[rows, 0 : 2 * NB]
            w0 = jnp.where(stay, w[rows, 0:NB].astype(F32), dot(take, s[:, COLS : COLS + NB])).astype(BF)
            w1 = jnp.where(stay, w[rows, NB : 2 * NB].astype(F32), dot(take, s[:, COLS + NB : COLS + 2 * NB]))
            low0 = dot(w0, ui[0]).astype(BF)
            x1 = (w1 - dot(low0, u0w[...])).astype(BF)
            dl[rows, 2 * NB : 3 * NB] = -low0
            dl[rows, 3 * NB : 4 * NB] = -dot(x1, ui[1]).astype(BF)
            return carry

        lax.fori_loop(0, ROWS // NB, body, 0)

    def uppers(c):
        cc = cols_of(c)
        u0 = dot(li[0], t[0:NB, cc]).astype(BF)
        su[2 * NB : 3 * NB, cc] = u0
        x1 = (t[NB : 2 * NB, cc].astype(F32) - dot(l0t[...], u0)).astype(BF)
        su[3 * NB : 4 * NB, cc] = dot(li[1], x1).astype(BF)

    def update(c):
        def body(i, carry):
            cc = pl.ds(pl.multiple_of(S_STARTS[c] + i * NB, NB), NB)
            stay = jnp.concatenate([keep[...], keep[...]], axis=1) > 0.5
            base = jnp.where(stay, a[:, cc].astype(F32), 0.0)
            ap[:, cc] = (base + dot(dl[...], su[:, cc])).astype(BF)
            return carry

        lax.fori_loop(0, S_WIDTHS[c] // NB, body, 0)
        cc = pl.ds(S_STARTS[c], S_WIDTHS[c])

        @pl.when(row == 0)
        def _():
            ap[0:NB, cc] = su[2 * NB : 3 * NB, cc]

        @pl.when(row == 1)
        def _():
            ap[0:NB, cc] = su[3 * NB : 4 * NB, cc]

        if c == 0:
            panel_out()

    def panel_out():
        @pl.when((z == 0) & (row > 0))
        def _():
            ap[0:NB, 0:NB] = -dl[0:NB, 2 * NB : 3 * NB]

        @pl.when((z == 1) & (row > 1))
        def _():
            ap[0:NB, 0:NB] = -dl[0:NB, 3 * NB : 4 * NB]

        @pl.when(z == 0)
        def _():
            ap[NB:ROWS, 0:NB] = -dl[NB:ROWS, 2 * NB : 3 * NB]

        @pl.when(z == 1)
        def _():
            ap[NB:ROWS, 0:NB] = -dl[NB:ROWS, 3 * NB : 4 * NB]

        @pl.when((z == 0) & (row == 0))
        def _():
            ap[0:NB, 0:NB] = t[0:NB, 0:NB]

        @pl.when((z == 0) & (row == 1))
        def _():
            ap[0:NB, 0:NB] = l0t[...]

        @pl.when((z == 1) & (row == 1))
        def _():
            ap[0:NB, 0:NB] = (t[NB : 2 * NB, 0:NB].astype(F32) - dot(l0t[...], u0w[...])).astype(BF)

    s_start()
    z_start(0)
    z_start(1)

    load_p.wait()
    p0r, p1r = piv_ref[0:1, :], piv_ref[1:2, :]
    p0c, p1c = turned(p0r), turned(p1r)
    i0 = lax.broadcasted_iota(jnp.int32, (NB, NB), 0)
    i1 = lax.broadcasted_iota(jnp.int32, (NB, NB), 1)
    hit = p1c == p0r
    src1 = jnp.where(
        jnp.max(hit.astype(jnp.int32), axis=1, keepdims=True) > 0,
        jnp.sum(jnp.where(hit, i1, 0), axis=1, keepdims=True),
        p1c,
    )
    src_other = jnp.where(core == 0, src1, p0c)
    src_mine = jnp.where(core == 0, p0c, src1)
    for b in range(ROWS // NB):
        glob_r = b * (NB * 2 * SIDE * SIDE) + row * NB + i1
        oh[0:NB, b * NB : (b + 1) * NB] = (src_other == glob_r).astype(F32).astype(BF)
        oh[NB : 2 * NB, b * NB : (b + 1) * NB] = (src_mine == glob_r).astype(F32).astype(BF)

    def places():
        inner = p0r == NB + i0
        out_in = jnp.sum(jnp.where(inner, p1c, 0), axis=0, keepdims=True)
        met = jnp.max(hit.astype(jnp.int32), axis=0, keepdims=True) > 0
        met_at = jnp.sum(jnp.where(hit, NB + i0, 0), axis=0, keepdims=True)
        dest0 = jnp.where(p0r < NB, p0r, jnp.where(p0r < 2 * NB, out_in, jnp.where(met, met_at, p0r)))
        back = p0c == NB + i1
        dest1 = jnp.where(
            jnp.max(back.astype(jnp.int32), axis=0, keepdims=True) > 0,
            jnp.sum(jnp.where(back, i0, 0), axis=0, keepdims=True),
            p1r,
        )
        for b in range(ROWS // NB):
            rows = pl.ds(b * NB, NB)
            glob_c = b * (NB * 2 * SIDE * SIDE) + row * NB + i0
            d0 = dest0 == glob_c
            d1 = dest1 == glob_c
            dl[rows, 0:NB] = d0.astype(F32).astype(BF)
            dl[rows, NB : 2 * NB] = d1.astype(F32).astype(BF)
            moved = jnp.max(jnp.maximum(d0.astype(F32), d1.astype(F32)), axis=1, keepdims=True)
            keep[rows, :] = jnp.broadcast_to(1.0 - moved, (NB, 128))

    names = ["S%d" % c for c in S_CHUNKS] + ["SE", "TE"] + ["T%d" % c for c in CHUNKS]
    gathers = {"n": gather_minor, "m": gather_major, "p": gather_pass, "c": gather_core, "g": gathered}
    stages = {
        "picks": picks, "core": reduce_core, "major": reduce_major, "minor": reduce_minor,
        "uppers": uppers, "update": update, "z": z_wave, "v": s_wave,
    }
    single = {
        "et": (e_start, 0), "es": (e_start, 1), "ert": (e_recv, 0), "ers": (e_recv, 1),
        "lowers": (lowers,), "lowtop": (lowtop,), "places": (places,),
    }
    steps = []
    for word in PLAN:
        if "." in word:
            steps.append((gathers[word[0]], names.index(word[2:])))
        elif word in single:
            steps.append(single[word])
        else:
            steps.append((stages[word[:-1]], int(word[-1])))
    for step, *which in steps:
        step(*which)

    s_end()
    z_end(0)
    z_end(1)
    e_end(0)
    e_end(1)
    for c in CHUNKS:
        x_copy(c).wait_send()
        for k in (1, 2, 3):
            r1_copy(c, k).wait_send()
            r2_copy(c, k).wait_send()
    for i in range(len(items)):
        c_copy(i).wait_send()
    for i in range(len(S_WIDTHS), len(items)):
        for k in (1, 2, 3):
            g1_copy(i, k).wait_send()
        for j in range(6):
            g2_copy(i, j).wait_send()


def per_device(a_stored, pivots, l_inverse, u_inverse):
    chunks = len(WIDTHS)
    n_items = 2 + chunks + len(S_WIDTHS)
    dma = pltpu.SemaphoreType.DMA
    hbm = pl.BlockSpec(memory_space=pltpu.HBM)
    scratch = [
        pltpu.VMEM((ROWS, COLS), BF),
        pltpu.VMEM((2 * NB, COLS + NB), BF),
        pltpu.VMEM((4 * NB, COLS + 2 * NB), BF),
        pltpu.VMEM((NB, COLS), BF),
        pltpu.VMEM((NB, COLS), BF),
        pltpu.VMEM((NB, COLS), BF),
        pltpu.VMEM((3, BIG, COLS), BF),
        pltpu.VMEM((BIG, COLS), BF),
        pltpu.VMEM((3, SHARD, COLS), BF),
        pltpu.VMEM((ROWS, 2 * NB), BF),
        pltpu.VMEM((ROWS, 4 * NB), BF),
        pltpu.VMEM((2 * NB, ROWS), BF),
        pltpu.VMEM((ROWS, 128), F32),
        pltpu.VMEM((NB, NB), BF),
        pltpu.VMEM((NB, NB), BF),
        pltpu.VMEM((2, NB, NB), BF),
        pltpu.VMEM((2, NB, NB), BF),
        pltpu.VMEM((2, NB), jnp.int32),
        dma((6,)), dma((chunks,)),
        dma((chunks,)), dma((chunks,)),
        dma((chunks, 3)), dma((chunks, 3)),
        dma((chunks, 3)), dma((chunks, 3)),
        dma((2, len(S_WIDTHS), 4)), dma((2, len(S_WIDTHS))),
        dma((n_items, 3)), dma((n_items, 3)),
        dma((n_items, 6)), dma((n_items, 6)),
        dma((n_items,)), dma((n_items,)),
        dma((2, 3, 2)), dma((2, 3)),
        dma((2, ZS - 1)), dma((2, 2)),
    ]
    return pl.pallas_call(
        kernel,
        out_shape=jax.ShapeDtypeStruct((ROWS, COLS), BF),
        in_specs=[hbm] * 4,
        out_specs=pl.BlockSpec(memory_space=pltpu.VMEM),
        scratch_shapes=scratch,
        compiler_params=pltpu.CompilerParams(
            collective_id=0, has_side_effects=True, vmem_limit_bytes=48 * 2**20
        ),
        name="panels",
    )(a_stored, pivots, l_inverse, u_inverse)


def solution(mesh):
    in_specs = (P("row", "col"), P(), P(), P())
    out_specs = P("row", "col")
    return jax.shard_map(
        per_device, mesh=mesh, in_specs=in_specs, out_specs=out_specs, check_vma=False
    )
```

time: 94.8 us -> 72.2 us (0.76)
  the two profiles are of different devices: /device:TPU:160 before, /device:TPU:1 now
where the time goes in v2:
time: 72.2 us; the launch traced here: 71.7 us
  Pallas kernels  66.9 us (93%)
  local copies, waits for them, and re-layouts  4.77 us (7%)
    pallas_call x1, Pallas kernels, per_device(): pl.pallas_call(kernel, out_shape=jax.ShapeDtypeStruct((ROWS, COLS), BF),...  66.9 us
    unnamed x7, local copies, waits for them, and re-layouts  4.77 us

profile of v2, /device:TPU:1, one launch (start us, length us, event | category | flops | bytes accessed | tf_op | source)
XLA Modules:
  0.0 71.7 jit_solution(17995167390622232110)
XLA Ops:
  0.0 0.0 copy-start
  0.0 0.9 %copy-done = bf16[2,256,256]{2,1,0:T(8,128)(2,1)S(1)} copy-done((bf16[2,256,256]{2,1,0:T(8,128)(2,1)S(1)}, bf16[2,256,256]{2,1,0:T(8,128)(2,1)}, u32[]{:S(2)}) %copy-start) | copy-done | bytes 262168
  1.0 0.0 copy-start.1
  1.0 0.9 %copy-done.1 = bf16[2,256,256]{2,1,0:T(8,128)(2,1)S(1)} copy-done((bf16[2,256,256]{2,1,0:T(8,128)(2,1)S(1)}, bf16[2,256,256]{2,1,0:T(8,128)(2,1)}, u32[]{:S(2)}) %copy-start.1) | copy-done | bytes 262168
  1.9 0.0 copy-start.2
  1.9 0.7 copy-done.2
  2.6 66.9 %panels.1 = bf16[768,3072]{1,0:T(8,128)(2,1)S(1)} custom-call(bf16[768,3072]{1,0:T(8,128)(2,1)} %a_hbm.1, s32[2,256]{1,0:T(2,128)S(1)} %copy-done.2, bf16[2,256,256]{2,1,0:T(8,128)(2,1)S(1)} %copy-done, bf16[2,256,256]{2,1,0:T(8,128)(2,1)S(1)} %copy-done.1), custom_call_target="tpu_custom_call" | custom-call | tf_op jit(solution)/shard_map/panels/pallas_call | solution.py:577
  69.5 2.2 %copy.6 = bf16[768,3072]{1,0:T(8,128)(2,1)} copy(bf16[768,3072]{1,0:T(8,128)(2,1)S(1)} %panels.1) | data formatting | bytes 9437184
Async XLA Ops:
  0.0 0.9 %copy-start = (bf16[2,256,256]{2,1,0:T(8,128)(2,1)S(1)}, bf16[2,256,256]{2,1,0:T(8,128)(2,1)}, u32[]{:S(2)}) copy-start(bf16[2,256,256]{2,1,0:T(8,128)(2,1)} %li_hbm.1) | copy-start | bytes 786436
  1.0 0.9 %copy-start.1 = (bf16[2,256,256]{2,1,0:T(8,128)(2,1)S(1)}, bf16[2,256,256]{2,1,0:T(8,128)(2,1)}, u32[]{:S(2)}) copy-start(bf16[2,256,256]{2,1,0:T(8,128)(2,1)} %ui_hbm.1) | copy-start | bytes 786436
  1.9 0.7 copy-start.2

commit v3 on v2

--- a/solution.py
+++ b/solution.py
@@ -15,7 +15,7 @@
 WIDTHS = (768, 768, 768, 768)
 STARTS = tuple(sum(WIDTHS[:c]) for c in range(len(WIDTHS)))
 CHUNKS = range(len(WIDTHS))
-S_WIDTHS = (256, 768, 768, 768, 512)
+S_WIDTHS = (768, 768, 768, 768)
 S_STARTS = tuple(sum(S_WIDTHS[:c]) for c in range(len(S_WIDTHS)))
 S_CHUNKS = range(len(S_WIDTHS))
 TREE = (
@@ -26,13 +26,13 @@
 STEP_X, STEP_Y = (1, 0, -1, 0), (0, 1, 0, -1)
 HALF = NB // 2
 PLAN = (
-    "v1", "picks0", "picks1", "v2", "core0", "z1", "core1", "picks2", "v3", "picks3", "places", "major0", "core2",
-    "z2", "major1", "minor0", "n.T0", "et", "v4", "core3", "z3", "major2", "ert", "n.TE", "m.T0", "v5", "minor1",
-    "es", "n.T1", "m.TE", "p.T0", "major3", "z4", "c.S0", "ers", "n.SE", "minor2", "n.T2", "p.TE", "m.T1", "c.T0",
-    "v6", "minor3", "m.SE", "c.TE", "p.T1", "n.T3", "z5", "g.TE", "g.T0", "lowtop", "p.SE", "m.T2", "c.S1", "c.T1",
-    "v7", "c.S2", "m.T3", "uppers0", "c.SE", "p.T2", "g.T1", "uppers1", "z6", "g.S0", "p.T3", "g.S1", "g.S2",
-    "g.SE", "lowers", "c.T2", "v8", "update0", "update1", "g.T2", "c.T3", "uppers2", "c.S3", "v9", "c.S4",
-    "update2", "g.T3", "uppers3", "g.S3", "update3", "g.S4", "update4",
+    "picks0", "v1", "picks1", "z1", "es", "core0", "picks2", "v2", "core1", "picks3", "places", "z2", "ers", "n.SE",
+    "major0", "core2", "v3", "major1", "core3", "minor0", "n.T0", "et", "z3", "major2", "ert", "n.TE", "v4", "m.SE",
+    "minor1", "major3", "m.T0", "minor2", "z4", "m.TE", "n.T1", "n.T2", "p.SE", "v5", "c.S0", "p.T0", "p.TE",
+    "minor3", "n.T3", "m.T1", "m.T2", "z5", "c.SE", "c.TE", "c.T0", "g.SE", "g.S0", "v6", "c.S1", "p.T1", "m.T3",
+    "g.TE", "lowtop", "g.T0", "uppers0", "p.T2", "z6", "lowers", "c.T1", "p.T3", "g.S1", "v7", "c.S2", "update0",
+    "c.T2", "g.T1", "uppers1", "g.S2", "c.T3", "update1", "g.T2", "uppers2", "v8", "c.S3", "g.T3", "update2",
+    "uppers3", "g.S3", "update3",
 )
 BIG = SIDE * 16
 SHARD = 16
@@ -53,10 +53,10 @@
 
 def kernel(
     a_hbm, piv_hbm, li_hbm, ui_hbm, ap,
-    a, t, su, ps, po, xr, r1, q, r2, w, dl, oh, keep, l0t, u0w, li, ui, piv_ref,
+    a, t, su, ps, po, xr, r1, q, r2, w, dl, oh, keep, se, l0t, u0w, li, ui, piv_ref,
     load_sem, part_sem,
     x_ss, x_rs, r1_ss, r1_rs, r2_ss, r2_rs, v_ss, v_rs,
-    g1_ss, g1_rs, g2_ss, g2_rs, c_ss, c_rs, z_ss, z_rs, e_ss, e_rs,
+    g1_ss, g1_rs, g2_ss, g2_rs, c_ss, c_rs, z_ss, z_rs, e_ss, e_rs, q_ss, q_rs,
 ):
     row = lax.axis_index("row")
     z = lax.axis_index("col")
@@ -103,7 +103,21 @@
     for dev in partners:
         pl.semaphore_signal(barrier, inc=1, device_id=dev, device_id_type=MESH)
 
-    pl.semaphore_wait(barrier, len(partners))
+    root = (m == 0) & (n == 0)
+    off_lines = (m != 0) & (n != 0)
+
+    @pl.when(root)
+    def _():
+        for mm in range(1, SIDE):
+            for nn in range(1, SIDE):
+                pl.semaphore_signal(barrier, inc=1, device_id=at(mm, nn), device_id_type=MESH)
+
+    @pl.when(off_lines)
+    def _():
+        pl.semaphore_signal(barrier, inc=1, device_id=at(0, 0), device_id_type=MESH)
+
+    more = jnp.where(root, (SIDE - 1) * (SIDE - 1), 0) + jnp.where(off_lines, 1, 0)
+    pl.semaphore_wait(barrier, len(partners) + more)
 
     mine = core * NB
 
@@ -129,21 +143,27 @@
             rel = lax.rem(z - blk + ZS, ZS)
             for b in range(ROWS // NB):
                 hops = wave - b
-                if 1 <= hops <= 4:
+                if 1 <= hops <= 3:
 
                     @pl.when(rel == hops)
                     def _():
                         z_copy(blk, b, 1, 0, False).wait_recv()
-                        if hops < 4:
-                            z_copy(blk, b, 1, 0, False).start()
-
-                if 1 <= hops <= 3:
+                        z_copy(blk, b, 1, 0, False).start()
+
+                if 1 <= hops <= 2:
 
                     @pl.when(rel == ZS - hops)
                     def _():
                         z_copy(blk, b, 1, 0, False).wait_recv()
-                        if hops < 3:
-                            z_copy(blk, b, -1, 1, False).start()
+                        z_copy(blk, b, -1, 1, False).start()
+
+    def z_last(blk):
+        rel = lax.rem(z - blk + ZS, ZS)
+
+        @pl.when((rel == 4) | (rel == 5))
+        def _():
+            for b in range(ROWS // NB):
+                z_copy(blk, b, 1, 0, False).wait_recv()
 
     def z_end(blk):
         rel = lax.rem(z - blk + ZS, ZS)
@@ -168,7 +188,7 @@
     )
     flip = 1 - 2 * core
 
-    depths, passes = [], []
+    depths, passes, inner = [], [], []
     for sign in (1, -1):
         px = lax.rem(sign * m + SIDE, SIDE)
         py = lax.rem(sign * flip * n + SIDE, SIDE)
@@ -178,6 +198,7 @@
             depth = depth + jnp.where((px == x) & (py == y), h, 0)
             go[way] = go[way] | ((px == (x - STEP_X[way]) % SIDE) & (py == (y - STEP_Y[way]) % SIDE))
         depths.append(depth)
+        inner.append(go[0] | go[1] | go[2] | go[3])
         passes.append(go)
 
     def v_copy(tree, b, way, first=False):
@@ -203,7 +224,7 @@
                 continue
             for tree in range(2):
 
-                @pl.when(depths[tree] == hops)
+                @pl.when((depths[tree] == hops) & inner[tree])
                 def _():
                     v_copy(tree, b, 0).wait_recv()
                     for way in range(4):
@@ -219,6 +240,13 @@
             def _():
                 own_rows.wait()
 
+    def s_leaf(b):
+        for tree in range(2):
+
+            @pl.when(jnp.logical_not(inner[tree]))
+            def _():
+                v_copy(tree, b, 0).wait_recv()
+
     def s_end():
         for tree in range(2):
             for b in S_CHUNKS:
@@ -230,18 +258,50 @@
 
     bufs = (t, s)
 
+    def q_copy(i):
+        mm, nn = (i + 1) // SIDE, (i + 1) % SIDE
+        rows = pl.ds(mm * BIG + nn * SHARD, SHARD)
+        return send(a_hbm.at[rows, pl.ds(0, NB)], se, q_ss.at[i], q_rs, at(mm, nn))
+
+    own_shard = pltpu.make_async_copy(a_hbm.at[pl.ds(0, SHARD), pl.ds(0, NB)], se, load_sem.at[6])
+
+    def q_start():
+        @pl.when(root & (z < 2))
+        def _():
+            for i in range(SIDE * SIDE - 1):
+                q_copy(i).start()
+            own_shard.start()
+
+    def q_wait():
+        @pl.when(jnp.logical_not(root) & (z < 2))
+        def _():
+            q_copy(0).wait_recv()
+
+        @pl.when(root & (z < 2))
+        def _():
+            own_shard.wait()
+
+    def q_end():
+        @pl.when(root & (z < 2))
+        def _():
+            for i in range(SIDE * SIDE - 1):
+                q_copy(i).wait_send()
+
     def e_copy(kind, blk, k):
         rows = shard(m, n)
         buf = bufs[kind]
         to = COLS + blk * NB if kind else COLS
+        src = se if kind else buf.at[rows, pl.ds(0, NB)]
         return send(
-            buf.at[rows, pl.ds(0, NB)], buf.at[rows, pl.ds(to, NB)], e_ss.at[kind, k - 1], e_rs.at[kind, blk], along(k)
+            src, buf.at[rows, pl.ds(to, NB)], e_ss.at[kind, k - 1], e_rs.at[kind, blk], along(k)
         )
 
     def e_sources(kind):
         return ((0, z == 0), (1, z == 1)) if kind else ((0, z == 1 - core),)
 
     def e_start(kind):
+        if kind:
+            q_wait()
         for blk, here in e_sources(kind):
 
             @pl.when(here)
@@ -249,7 +309,7 @@
                 for k in (4, 3, 5, 2, 6, 1, 7):
                     e_copy(kind, blk, k).start()
                 to = COLS + blk * NB if kind else COLS
-                bufs[kind][shard(m, n), to : to + NB] = bufs[kind][shard(m, n), 0:NB]
+                bufs[kind][shard(m, n), to : to + NB] = se[...] if kind else t[shard(m, n), 0:NB]
 
     def e_recv(kind):
         for blk, here in e_sources(kind):
@@ -362,7 +422,9 @@
         return send(part, part, c_ss.at[i], c_rs.at[i], sibling)
 
     def gather_core(i):
-        if i >= len(S_WIDTHS):
+        if i < len(S_WIDTHS):
+            s_leaf(i)
+        else:
             for j in (2, 3, 4, 5):
                 g2_copy(i, j).wait_recv()
         c_copy(i).start()
@@ -378,6 +440,7 @@
 
     def lowers():
         for blk in range(2):
+            z_last(blk)
 
             @pl.when(z == blk)
             def _():
@@ -455,6 +518,7 @@
         def _():
             ap[0:NB, 0:NB] = (t[NB : 2 * NB, 0:NB].astype(F32) - dot(l0t[...], u0w[...])).astype(BF)
 
+    q_start()
     s_start()
     z_start(0)
     z_start(1)
@@ -478,8 +542,8 @@
         oh[NB : 2 * NB, b * NB : (b + 1) * NB] = (src_mine == glob_r).astype(F32).astype(BF)
 
     def places():
-        inner = p0r == NB + i0
-        out_in = jnp.sum(jnp.where(inner, p1c, 0), axis=0, keepdims=True)
+        hit_top = p0r == NB + i0
+        out_in = jnp.sum(jnp.where(hit_top, p1c, 0), axis=0, keepdims=True)
         met = jnp.max(hit.astype(jnp.int32), axis=0, keepdims=True) > 0
         met_at = jnp.sum(jnp.where(hit, NB + i0, 0), axis=0, keepdims=True)
         dest0 = jnp.where(p0r < NB, p0r, jnp.where(p0r < 2 * NB, out_in, jnp.where(met, met_at, p0r)))
@@ -520,6 +584,7 @@
     for step, *which in steps:
         step(*which)
 
+    q_end()
     s_end()
     z_end(0)
     z_end(1)
@@ -558,12 +623,13 @@
         pltpu.VMEM((ROWS, 4 * NB), BF),
         pltpu.VMEM((2 * NB, ROWS), BF),
         pltpu.VMEM((ROWS, 128), F32),
+        pltpu.VMEM((SHARD, NB), BF),
         pltpu.VMEM((NB, NB), BF),
         pltpu.VMEM((NB, NB), BF),
         pltpu.VMEM((2, NB, NB), BF),
         pltpu.VMEM((2, NB, NB), BF),
         pltpu.VMEM((2, NB), jnp.int32),
-        dma((6,)), dma((chunks,)),
+        dma((7,)), dma((chunks,)),
         dma((chunks,)), dma((chunks,)),
         dma((chunks, 3)), dma((chunks, 3)),
         dma((chunks, 3)), dma((chunks, 3)),
@@ -573,6 +639,7 @@
         dma((n_items,)), dma((n_items,)),
         dma((2, 3, 2)), dma((2, 3)),
         dma((2, ZS - 1)), dma((2, 2)),
+        dma((SIDE * SIDE - 1,)), dma,
     ]
     return pl.pallas_call(
         kernel,

time: 72.2 us -> 67.4 us (0.934)
  Pallas kernels: 66.9 us -> 62.5 us
    pallas_call x1, Pallas kernels: 66.9 us -> 62.5 us  [per_device(): pl.pallas_call(kernel, out_shape=jax.ShapeDtypeStruct((ROWS, COLS), BF),...]
where the time goes in v3:
time: 67.4 us; the launch traced here: 67.2 us
  Pallas kernels  62.5 us (93%)
  local copies, waits for them, and re-layouts  4.77 us (7%)
    pallas_call x1, Pallas kernels, per_device(): pl.pallas_call(kernel, out_shape=jax.ShapeDtypeStruct((ROWS, COLS), BF),...  62.5 us
    unnamed x7, local copies, waits for them, and re-layouts  4.77 us

profile of v3, /device:TPU:1, one launch (start us, length us, event | category | flops | bytes accessed | tf_op | source)
XLA Modules:
  0.0 67.2 jit_solution(12533010835091623728)
XLA Ops:
  0.0 0.0 copy-start
  0.0 0.9 %copy-done = bf16[2,256,256]{2,1,0:T(8,128)(2,1)S(1)} copy-done((bf16[2,256,256]{2,1,0:T(8,128)(2,1)S(1)}, bf16[2,256,256]{2,1,0:T(8,128)(2,1)}, u32[]{:S(2)}) %copy-start) | copy-done | bytes 262168
  1.0 0.0 copy-start.1
  1.0 0.9 %copy-done.1 = bf16[2,256,256]{2,1,0:T(8,128)(2,1)S(1)} copy-done((bf16[2,256,256]{2,1,0:T(8,128)(2,1)S(1)}, bf16[2,256,256]{2,1,0:T(8,128)(2,1)}, u32[]{:S(2)}) %copy-start.1) | copy-done | bytes 262168
  1.9 0.0 copy-start.2
  1.9 0.7 %copy-done.2 = s32[2,256]{1,0:T(2,128)S(1)} copy-done((s32[2,256]{1,0:T(2,128)S(1)}, s32[2,256]{1,0:T(2,128)}, u32[]{:S(2)}) %copy-start.2) | copy-done | bytes 2072
  2.6 62.5 %panels.1 = bf16[768,3072]{1,0:T(8,128)(2,1)S(1)} custom-call(bf16[768,3072]{1,0:T(8,128)(2,1)} %a_hbm.1, s32[2,256]{1,0:T(2,128)S(1)} %copy-done.2, bf16[2,256,256]{2,1,0:T(8,128)(2,1)S(1)} %copy-done, bf16[2,256,256]{2,1,0:T(8,128)(2,1)S(1)} %copy-done.1), custom_call_target="tpu_custom_call" | custom-call | tf_op jit(solution)/shard_map/panels/pallas_call | solution.py:644
  65.1 2.2 %copy.6 = bf16[768,3072]{1,0:T(8,128)(2,1)} copy(bf16[768,3072]{1,0:T(8,128)(2,1)S(1)} %panels.1) | data formatting | bytes 9437184
Async XLA Ops:
  0.0 0.9 %copy-start = (bf16[2,256,256]{2,1,0:T(8,128)(2,1)S(1)}, bf16[2,256,256]{2,1,0:T(8,128)(2,1)}, u32[]{:S(2)}) copy-start(bf16[2,256,256]{2,1,0:T(8,128)(2,1)} %li_hbm.1) | copy-start | bytes 786436
  1.0 0.9 %copy-start.1 = (bf16[2,256,256]{2,1,0:T(8,128)(2,1)S(1)}, bf16[2,256,256]{2,1,0:T(8,128)(2,1)}, u32[]{:S(2)}) copy-start(bf16[2,256,256]{2,1,0:T(8,128)(2,1)} %ui_hbm.1) | copy-start | bytes 786436
  1.9 0.7 %copy-start.2 = (s32[2,256]{1,0:T(2,128)S(1)}, s32[2,256]{1,0:T(2,128)}, u32[]{:S(2)}) copy-start(s32[2,256]{1,0:T(2,128)} %piv_hbm.1) | copy-start | bytes 6148

commit v4 on v3

--- a/solution.py
+++ b/solution.py
@@ -641,6 +641,7 @@
         dma((2, ZS - 1)), dma((2, 2)),
         dma((SIDE * SIDE - 1,)), dma,
     ]
+    small = [pltpu.with_memory_space_constraint(v, pltpu.HBM) for v in (pivots, l_inverse, u_inverse)]
     return pl.pallas_call(
         kernel,
         out_shape=jax.ShapeDtypeStruct((ROWS, COLS), BF),
@@ -651,7 +652,7 @@
             collective_id=0, has_side_effects=True, vmem_limit_bytes=48 * 2**20
         ),
         name="panels",
-    )(a_stored, pivots, l_inverse, u_inverse)
+    )(a_stored, *small)
 
 
 def solution(mesh):

time: 67.4 us -> 64.6 us (0.958)
  local copies, waits for them, and re-layouts: 4.77 us -> 2.19 us
    unnamed x7 -> x1, local copies, waits for them, and re-layouts: 4.77 us -> 2.19 us
where the time goes in v4:
time: 64.6 us
  Pallas kernels  62.4 us (97%)
  local copies, waits for them, and re-layouts  2.19 us (3%)
    pallas_call x1, Pallas kernels, per_device(): pl.pallas_call(kernel, out_shape=jax.ShapeDtypeStruct((ROWS, COLS), BF),...  62.4 us
    unnamed x1, local copies, waits for them, and re-layouts  2.19 us

profile of v4, /device:TPU:1, one launch (start us, length us, event | category | flops | bytes accessed | tf_op | source)
XLA Modules:
  0.0 64.6 jit_solution(13586846682460210141)
XLA Ops:
  0.0 62.4 %panels.1 = bf16[768,3072]{1,0:T(8,128)(2,1)S(1)} custom-call(bf16[768,3072]{1,0:T(8,128)(2,1)} %a_hbm.1, s32[2,256]{1,0:T(2,128)} %piv_hbm.1, bf16[2,256,256]{2,1,0:T(8,128)(2,1)} %li_hbm.1, bf16[2,256,256]{2,1,0:T(8,128)(2,1)} %ui_hbm.1), custom_call_target="tpu_custom_call" | custom-call | tf_op jit(solution)/shard_map/panels/pallas_call | solution.py:645
  62.4 2.2 %copy.6 = bf16[768,3072]{1,0:T(8,128)(2,1)} copy(bf16[768,3072]{1,0:T(8,128)(2,1)S(1)} %panels.1) | data formatting | bytes 9437184

commit v5 on v4

--- a/solution.py
+++ b/solution.py
@@ -31,7 +31,7 @@
     "minor1", "major3", "m.T0", "minor2", "z4", "m.TE", "n.T1", "n.T2", "p.SE", "v5", "c.S0", "p.T0", "p.TE",
     "minor3", "n.T3", "m.T1", "m.T2", "z5", "c.SE", "c.TE", "c.T0", "g.SE", "g.S0", "v6", "c.S1", "p.T1", "m.T3",
     "g.TE", "lowtop", "g.T0", "uppers0", "p.T2", "z6", "lowers", "c.T1", "p.T3", "g.S1", "v7", "c.S2", "update0",
-    "c.T2", "g.T1", "uppers1", "g.S2", "c.T3", "update1", "g.T2", "uppers2", "v8", "c.S3", "g.T3", "update2",
+    "c.T2", "g.T1", "uppers1", "g.S2", "c.T3", "update1", "g.T2", "v8", "c.S3", "uppers2", "g.T3", "update2",
     "uppers3", "g.S3", "update3",
 )
 BIG = SIDE * 16

time: 64.6 us -> 64.6 us (level)
  no operation moved by 1% of the time
where the time goes in v5:
time: 64.6 us
  Pallas kernels  62.4 us (97%)
  local copies, waits for them, and re-layouts  2.19 us (3%)
    pallas_call x1, Pallas kernels, per_device(): pl.pallas_call(kernel, out_shape=jax.ShapeDtypeStruct((ROWS, COLS), BF),...  62.4 us
    unnamed x1, local copies, waits for them, and re-layouts  2.19 us

profile of v5, /device:TPU:1, one launch (start us, length us, event | category | flops | bytes accessed | tf_op | source)
XLA Modules:
  0.0 64.6 jit_solution(15750671946831879968)
XLA Ops:
  0.0 62.4 %panels.1 = bf16[768,3072]{1,0:T(8,128)(2,1)S(1)} custom-call(bf16[768,3072]{1,0:T(8,128)(2,1)} %a_hbm.1, s32[2,256]{1,0:T(2,128)} %piv_hbm.1, bf16[2,256,256]{2,1,0:T(8,128)(2,1)} %li_hbm.1, bf16[2,256,256]{2,1,0:T(8,128)(2,1)} %ui_hbm.1), custom_call_target="tpu_custom_call" | custom-call | tf_op jit(solution)/shard_map/panels/pallas_call | solution.py:645
  62.4 2.2 %copy.6 = bf16[768,3072]{1,0:T(8,128)(2,1)} copy(bf16[768,3072]{1,0:T(8,128)(2,1)S(1)} %panels.1) | data formatting | bytes 9437184
